TPU v7x, 32 devices: a whole 2x2x4 slice. The times are simulated.
32 devices in a mesh: gx: 16 (over z, y, core), gy: 2 (over x).
Axes of the slice: x: 2, y: 2, z: 4, core: 2. Of those that a mesh axis runs over, the one named last changes fastest.
Arguments:
- latents: int32 [768, 64, 32], P('gy', 'gx'), may hold values from 0 to 31
- actions: int32 [768, 64], P('gy', 'gx'), may hold values from 0 to 17
- segment_ids: int32 [768, 64], replicated, may hold values from 0 to 3, never falling along the last dimension, each value on 1 to 32 neighbouring positions
- cotangent: bfloat16 [768, 64, 512], P('gy', 'gx'), may hold values from -6 to 6
- stem_weight: bfloat16 [1024, 512], replicated, may hold values from -1 to 1
- action_table: bfloat16 [18, 512], replicated, may hold values from -1 to 1
- first_gain: float32 [512], replicated, may hold values from 0.5 to 1.5
- first_bias: float32 [512], replicated, may hold values from -1 to 1
- query_weight: bfloat16 [512, 512], P(None, 'gy'), may hold values from -0.25 to 0.25
- key_weight: bfloat16 [512, 512], P(None, 'gy'), may hold values from -0.25 to 0.25
- value_weight: bfloat16 [512, 512], P(None, 'gy'), may hold values from -0.25 to 0.25
- out_weight: bfloat16 [512, 512], P('gy'), may hold values from -1 to 1
- second_gain: float32 [512], replicated, may hold values from 0.5 to 1.5
- second_bias: float32 [512], replicated, may hold values from -1 to 1
- up_weight: bfloat16 [512, 2048], P(None, 'gy'), may hold values from -0.25 to 0.25
- up_bias: float32 [2048], P('gy'), may hold values from -1 to 1
- down_weight: bfloat16 [2048, 512], P('gy'), may hold values from -0.125 to 0.125
- down_bias: float32 [512], replicated, may hold values from -1 to 1
Outputs:
- output: bfloat16 [768, 64, 512], P('gy', 'gx')
- token_grad: bfloat16 [768, 64, 512], P('gy', 'gx')
- stem_grad: float32 [1024, 512], replicated
- action_grad: float32 [18, 512], replicated
- first_gain_grad: float32 [512], replicated
- first_bias_grad: float32 [512], replicated
- query_grad: float32 [512, 512], P(None, 'gy')
- key_grad: float32 [512, 512], P(None, 'gy')
- value_grad: float32 [512, 512], P(None, 'gy')
- out_grad: float32 [512, 512], P('gy')
- second_gain_grad: float32 [512], replicated
- second_bias_grad: float32 [512], replicated
- up_grad: float32 [512, 2048], P(None, 'gy')
- up_bias_grad: float32 [2048], P('gy')
- down_grad: float32 [2048, 512], P('gy')
- down_bias_grad: float32 [512], replicated
Inputs may be any that keep to these rules, and one draw needn't show every extreme that they name: `segment_ids`: along each sequence of 64 frames the segment id never falls; each segment holds 1 to 32 frames.
All inputs are finite; a program needn't handle non-finite values.
Results may differ from a plain program's by a relative error of at most 0.012.
Values may be sent and summed in bfloat16 or wider, within the bound.
A program may use at most 192 MiB of HBM per device.

v0:
```python
import jax
import jax.numpy as jnp
from jax import lax
from jax.sharding import PartitionSpec as P

HD = 64
EPSILON = 1e-05
FLOAT = jnp.float32
BFLOAT = jnp.bfloat16


def norm_rows(values, gain, bias):
    average = jnp.mean(values, axis=-1, keepdims=True)
    centred = values - average
    spread = jnp.mean(centred * centred, axis=-1, keepdims=True)
    return centred * lax.rsqrt(spread + EPSILON) * gain + bias


def inner(left, right):
    return lax.dot_general(left, right, (((0,), (0,)), ((), ())), preferred_element_type=FLOAT)


def outer(left, right):
    return lax.dot_general(left, right, (((1,), (1,)), ((), ())), preferred_element_type=FLOAT)


def product(left, right):
    return jnp.dot(left, right, preferred_element_type=FLOAT)


def split_heads(block):
    return block.reshape(block.shape[0], block.shape[1], -1, HD)


def block_probs(query_block, key_block, label_block):
    length = query_block.shape[1]
    scores = 0.125 * jnp.einsum(
        "sqhd,skhd->shqk",
        split_heads(query_block),
        split_heads(key_block),
        preferred_element_type=FLOAT,
    )
    place = jnp.arange(length)
    allowed = (label_block[:, :, None] == label_block[:, None, :]) & (
        place[:, None] >= place[None, :]
    )[None]
    return jax.nn.softmax(jnp.where(allowed[:, None], scores, -1e30), axis=-1)


def block_forward(pieces):
    query_block, key_block, value_block, label_block = pieces
    probs_low = block_probs(query_block, key_block, label_block).astype(BFLOAT)
    mixed = jnp.einsum(
        "shqk,skhd->sqhd", probs_low, split_heads(value_block), preferred_element_type=FLOAT
    )
    return mixed.reshape(query_block.shape[0], query_block.shape[1], -1).astype(BFLOAT)


def block_backward(pieces):
    query_block, key_block, value_block, label_block, grad_block = pieces
    probs = block_probs(query_block, key_block, label_block)
    grad_heads = split_heads(grad_block)
    grad_probs = jnp.einsum(
        "sqhd,skhd->shqk", grad_heads, split_heads(value_block), preferred_element_type=FLOAT
    )
    grad_probs = lax.optimization_barrier(grad_probs.astype(BFLOAT)).astype(FLOAT)
    centre = jnp.sum(probs * grad_probs, axis=-1, keepdims=True)
    grad_scores = (probs * (grad_probs - centre)).astype(BFLOAT)
    grad_query = 0.125 * jnp.einsum(
        "shqk,skhd->sqhd", grad_scores, split_heads(key_block), preferred_element_type=FLOAT
    )
    grad_key = 0.125 * jnp.einsum(
        "shqk,sqhd->skhd", grad_scores, split_heads(query_block), preferred_element_type=FLOAT
    )
    grad_value = jnp.einsum(
        "shqk,sqhd->skhd", probs.astype(BFLOAT), grad_heads, preferred_element_type=FLOAT
    )
    shape = (query_block.shape[0], query_block.shape[1], -1)
    return tuple(
        (item.reshape(shape).astype(BFLOAT) for item in (grad_query, grad_key, grad_value))
    )


def layer_pass(seq_tokens, seq_cot, seg_rows, weights):
    (
        first_gain,
        first_bias,
        query_weight,
        key_weight,
        value_weight,
        out_weight,
        second_gain,
        second_bias,
        up_weight,
        up_bias,
        down_weight,
        down_bias,
    ) = weights
    seqs, length, width = seq_tokens.shape
    rows = seqs * length
    block = min(512, rows)
    blocks = rows // block
    within = block // length
    scale = 0.5
    inputs = seq_tokens.reshape(rows, width).astype(FLOAT)
    normed_one = norm_rows(inputs, first_gain, first_bias).astype(BFLOAT)
    query = product(normed_one, query_weight).astype(BFLOAT)
    key_rows = product(normed_one, key_weight).astype(BFLOAT)
    value_rows = product(normed_one, value_weight).astype(BFLOAT)
    labels = seg_rows.reshape(blocks, within, length)

    def split_rows(array):
        return array.reshape(blocks, within, length, -1)

    mixed = lax.map(
        block_forward, (split_rows(query), split_rows(key_rows), split_rows(value_rows), labels)
    )
    mixed = mixed.reshape(rows, -1)
    branch = product(mixed, out_weight)
    branch = lax.psum(branch, "gy")
    resid = inputs + branch
    normed_two = norm_rows(resid, second_gain, second_bias).astype(BFLOAT)
    pre_act = product(normed_two, up_weight) + up_bias
    hidden = jax.nn.gelu(pre_act).astype(BFLOAT)
    out_part = scale * (resid + down_bias) + product(hidden, down_weight)
    cot_rows = seq_cot.reshape(rows, width)
    cot_float = cot_rows.astype(FLOAT)
    down_bias_part = jnp.sum(cot_float, axis=0)
    down_part = inner(hidden, cot_rows)
    d_hidden = outer(cot_rows, down_weight)
    act_input = product(normed_two, up_weight) + up_bias
    _, gelu_pull = jax.vjp(jax.nn.gelu, act_input)
    d_pre = gelu_pull(d_hidden)[0].astype(BFLOAT)
    up_bias_part = jnp.sum(d_pre.astype(FLOAT), axis=0)
    up_part = inner(normed_two, d_pre)
    d_normed_two = outer(d_pre, up_weight)
    d_normed_two = lax.psum(d_normed_two, "gy")
    _, second_pull = jax.vjp(norm_rows, resid, second_gain, second_bias)
    d_resid_norm, second_gain_part, second_bias_part = second_pull(d_normed_two)
    d_resid = cot_float + d_resid_norm
    d_branch = d_resid.astype(BFLOAT)
    out_part_grad = inner(mixed, d_branch)
    d_mixed = outer(d_branch, out_weight).astype(BFLOAT)
    d_query, d_key, d_value = lax.map(
        block_backward,
        (
            split_rows(query),
            split_rows(key_rows),
            split_rows(value_rows),
            labels,
            split_rows(d_mixed),
        ),
    )
    d_query = d_query.reshape(rows, -1)
    d_key = d_key.reshape(rows, -1)
    d_value = d_value.reshape(rows, -1)
    query_part = inner(normed_one, d_query)
    key_part = inner(normed_one, d_key)
    value_part = inner(normed_one, d_value)
    d_normed_one = (
        outer(d_query, query_weight) + outer(d_key, key_weight) + outer(d_value, value_weight)
    )
    _, first_pull = jax.vjp(norm_rows, inputs, first_gain, first_bias)
    d_input_norm, first_gain_part, first_bias_part = first_pull(d_normed_one)
    d_tokens_part = scale * d_resid + d_input_norm
    parts = (
        first_gain_part,
        first_bias_part,
        query_part,
        key_part,
        value_part,
        out_part_grad,
        second_gain_part,
        second_bias_part,
        up_part,
        up_bias_part,
        down_part,
        down_bias_part,
    )
    return (
        out_part.reshape(seqs, length, width),
        d_tokens_part.reshape(seqs, length, width),
        parts,
    )


def per_device(
    latents,
    actions,
    segment_ids,
    cotangent,
    stem_weight,
    action_table,
    first_gain,
    first_bias,
    query_weight,
    key_weight,
    value_weight,
    out_weight,
    second_gain,
    second_bias,
    up_weight,
    up_bias,
    down_weight,
    down_bias,
):
    half_seqs, local_len, groups = latents.shape
    frames = half_seqs * local_len
    classes = stem_weight.shape[0] // groups
    latent_hot = (latents[..., None] == jnp.arange(classes, dtype=jnp.int32)).reshape(
        frames, groups * classes
    )
    latent_hot = latent_hot.astype(BFLOAT)
    action_hot = (
        actions.reshape(frames, 1) == jnp.arange(action_table.shape[0], dtype=jnp.int32)[None, :]
    )
    action_hot = action_hot.astype(BFLOAT)
    stem = product(latent_hot, stem_weight) + product(action_hot, action_table)
    tokens = stem.astype(BFLOAT).reshape(half_seqs, local_len, -1)
    token_all, cot_all = (
        lax.all_gather(tokens, "gy", axis=0, tiled=True),
        lax.all_gather(cotangent, "gy", axis=0, tiled=True),
    )
    seq_tokens, seq_cot = (
        lax.all_to_all(token_all, "gx", split_axis=0, concat_axis=1, tiled=True),
        lax.all_to_all(cot_all, "gx", split_axis=0, concat_axis=1, tiled=True),
    )
    seqs = seq_tokens.shape[0]
    first_seq = lax.axis_index("gx") * seqs
    weights = (
        first_gain,
        first_bias,
        query_weight,
        key_weight,
        value_weight,
        out_weight,
        second_gain,
        second_bias,
        up_weight,
        up_bias,
        down_weight,
        down_bias,
    )
    seg_rows = lax.dynamic_slice_in_dim(segment_ids, first_seq, seqs, 0)
    out_seq, grad_seq, parts = layer_pass(seq_tokens, seq_cot, seg_rows, weights)
    out_moved, grad_moved = (
        lax.all_to_all(out_seq, "gx", split_axis=1, concat_axis=0, tiled=True),
        lax.all_to_all(grad_seq, "gx", split_axis=1, concat_axis=0, tiled=True),
    )
    out_frames, grad_frames = (
        lax.psum_scatter(out_moved, "gy", scatter_dimension=0, tiled=True),
        lax.psum_scatter(grad_moved, "gy", scatter_dimension=0, tiled=True),
    )
    output = out_frames.astype(BFLOAT)
    token_grad = grad_frames.astype(BFLOAT)
    width = stem_weight.shape[1]
    grad_flat = token_grad.reshape(frames, width)
    stem_part = inner(latent_hot, grad_flat)
    action_part = inner(action_hot, grad_flat)
    (
        first_gain_part,
        first_bias_part,
        query_part,
        key_part,
        value_part,
        out_part_grad,
        second_gain_part,
        second_bias_part,
        up_part,
        up_bias_part,
        down_part,
        down_bias_part,
    ) = parts
    stem_grad, action_grad, first_gain_grad, first_bias_grad = lax.psum(
        (stem_part, action_part, first_gain_part, first_bias_part), ("gx", "gy")
    )
    (
        query_grad,
        key_grad,
        value_grad,
        out_grad,
        second_gain_grad,
        second_bias_grad,
        up_grad,
        up_bias_grad,
        down_grad,
        down_bias_grad,
    ) = lax.psum(
        (
            query_part,
            key_part,
            value_part,
            out_part_grad,
            second_gain_part,
            second_bias_part,
            up_part,
            up_bias_part,
            down_part,
            down_bias_part,
        ),
        "gx",
    )
    return (
        output,
        token_grad,
        stem_grad,
        action_grad,
        first_gain_grad,
        first_bias_grad,
        query_grad,
        key_grad,
        value_grad,
        out_grad,
        second_gain_grad,
        second_bias_grad,
        up_grad,
        up_bias_grad,
        down_grad,
        down_bias_grad,
    )


def solution(mesh):
    return jax.shard_map(
        per_device,
        mesh=mesh,
        in_specs=(
            P("gy", "gx", None),
            P("gy", "gx"),
            P(),
            P("gy", "gx", None),
            P(),
            P(),
            P(),
            P(),
            P(None, "gy"),
            P(None, "gy"),
            P(None, "gy"),
            P("gy", None),
            P(),
            P(),
            P(None, "gy"),
            P("gy"),
            P("gy", None),
            P(),
        ),
        out_specs=(
            P("gy", "gx", None),
            P("gy", "gx", None),
            P(),
            P(),
            P(),
            P(),
            P(None, "gy"),
            P(None, "gy"),
            P(None, "gy"),
            P("gy", None),
            P(),
            P(),
            P(None, "gy"),
            P("gy"),
            P("gy", None),
            P(),
        ),
        check_vma=False,
    )
```

profile of v0, /device:TPU:0, one launch (start us, length us, event | category | flops | bytes accessed | tf_op | source)
XLA Modules:
  0.0 1381.9 jit_solution(16798744642058293899)
XLA Ops:
  8.6 9.8 eq.86
  18.4 19.9 %eq.87 = s32[1536,1024]{1,0:T(8,128)} reshape(s32[384,4,32,32]{3,2,1,0:T(8,128)} %eq.86) | data formatting | bytes 12582912 | tf_op jit(solution)/shard_map/eq | solution.py:210
  46.1 47.8 %all-gather.3.cloned.1.call-done = bf16[768,4,512]{2,1,0:T(4,128)(2,1)} async-done(((bf16[384,4,512]{2,1,0:T(4,128)(2,1)}), bf16[768,4,512]{2,1,0:T(4,128)(2,1)}) %all-gather.3.cloned.1.call-update) | async-done | bytes 3145744 | tf_op jit(solution)/shard_map/all_gather | solution.py:221
  101.8 57.1 %all-to-all-done = bf16[768,4,512]{2,1,0:T(4,128)(2,1)} async-done(((bf16[768,4,512]{2,1,0:T(4,128)(2,1)}), bf16[768,4,512]{2,1,0:T(4,128)(2,1)}, u32[]{:S(2)}, u32[]{:S(2)}) %all-to-all-start) | async-done | bytes 3145760 | tf_op jit(solution)/shard_map/all_to_all | solution.py:225
  166.9 6.3 copy_bitcast_fusion
  174.3 7.6 reshape.397
  193.5 43.5 %while.24 = (s32[]{:T(128)}, bf16[6,8,64,256]{3,2,1,0:T(8,128)(2,1)}, bf16[6,8,64,256]{3,2,1,0:T(8,128)(2,1)}, s32[6,8,64]{2,1,0:T(8,128)S(1)}, bf16[6,8,64,256]...) while((s32[]{:T(128)}, bf16[6,8,64,256]{3,2,1,0:T(8,128)(2,1)}, ...), condition=%wide.region_5.6_spmd, body=%wide.region_2.5_spmd.sunk | while | flops 34674816 | bytes 9009781 | solution.py:115
  242.1 85.4 %all_to_all.60 = bf16[768,4,512]{2,1,0:T(4,128)(2,1)S(1)} all-to-all(bf16[768,4,512]{2,1,0:T(4,128)(2,1)} %all-gather.5.cloned.1.call-done), channel_id=1, replica_groups=mesh['gx'=16,'gy'=2] {'gx'}, dimensions={0} | all-to-all | bytes 6291456 | tf_op jit(solution)/shard_map/all_to_all | solution.py:226
  338.2 67.0 %all-reduce.12.cloned.1.call-done = f32[3072,512]{1,0:T(8,128)} async-done(((f32[3072,512]{1,0:T(8,128)}), f32[3072,512]{1,0:T(8,128)}) %all-reduce.12.cloned.1.call-update) | async-done | bytes 6291472 | tf_op jit(solution)/shard_map/psum | solution.py:120
  412.7 9.9 multiply_convert_fusion
  422.7 13.3 convert_reduce_fusion
  438.6 5.8 fusion.47
  445.0 9.6 multiply_add_fusion
  454.7 6.4 copy.108
  461.0 6.1 all-to-all-start.1
  467.1 130.6 %all-reduce.14.cloned.1.call-done = f32[3072,512]{1,0:T(8,128)} async-done(((f32[3072,512]{1,0:T(8,128)}), f32[3072,512]{1,0:T(8,128)}) %all-reduce.14.cloned.1.call-update) | async-done | bytes 6291472 | tf_op jit(solution)/shard_map/psum | solution.py:137
  597.7 6.1 multiply_reduce_fusion
  618.5 89.6 %while.25 = (s32[]{:T(128)}, bf16[6,8,64,256]{3,2,1,0:T(8,128)(2,1)}, bf16[6,8,64,256]{3,2,1,0:T(8,128)(2,1)}, bf16[6,8,64,256]{3,2,1,0:T(8,128)(2,1)}, bf16[6,8...) while((s32[]{:T(128)}, ...), condition=%wide.region_17.18_spmd, body=%wide.region_13.17_spmd.sunk | while | flops 86839424 | bytes 17955988 | solution.py:144
  716.4 8.2 multiply_reduce_fusion.1
  731.8 6.3 copy.113
  738.1 5.8 all-to-all-start.3
  744.0 9.9 iota_compare_fusion.2
  753.9 15.2 %eq.98 = pred[1536,1024]{1,0:T(32,128)(4,1)} reshape(pred[384,4,32,32]{3,2,1,0:T(32,128)(4,1)} %iota_compare_fusion.2) | data formatting | bytes 3145728 | tf_op jit(solution)/shard_map/eq | solution.py:210
  781.7 8.6 fusion.55
  790.3 7.8 fusion.39
  805.8 9.7 copy.109
  815.5 58.3 %all-to-all-done.3 = f32[48,64,512]{2,0,1:T(8,128)} async-done(((f32[48,64,512]{2,0,1:T(8,128)}), f32[48,64,512]{2,0,1:T(8,128)}, u32[]{:S(2)}, u32[]{:S(2)}) %all-to-all-start.3) | async-done | bytes 6291488 | tf_op jit(solution)/shard_map/all_to_all | solution.py:248
  873.8 9.6 copy.114
  883.4 290.4 %all-reduce.19 = (bf16[768,4,512]{2,1,0:T(4,128)(2,1)}, bf16[768,4,512]{2,1,0:T(4,128)(2,1)}) all-reduce(f32[768,4,512]{2,1,0:T(4,128)} %bitcast.176, f32[768,4,512]{2,1,0:T(4,128)} %bitcast.177), channel_id=2, replica_groups=mesh['gx'=16,'gy'=2] {'gy'}, use_global_device_ids=true, to_apply=%region_9.10.clone | all-reduce | flops 3145728 | bytes 18874368
  1187.1 102.3 %all-reduce.3 = (f32[512]{0:T(512)}, f32[512]{0:T(512)}, f32[1024]{0:T(1024)}, f32[512]{0:T(512)}) all-reduce(f32[512]{0:T(512)S(1)} %get-tuple-element.146, f32[512]{0:T(512)S(1)} %get-tuple-element.150, f32[1024]{0:T(1024)S(1)} %copy-done.49, f32[512]{0:T(512)S(1)} %convert_reduce_fusion.1), channel_id=1, replica_groups=mesh['gx'=16,'gy'=2] {'gx'}, use_global_device_ids=true, to_apply=%region_32.33 | all-reduce | flops 2560 | bytes 20480 | tf_op jit(solution)/shard_map/psum | solution.py:288
  1289.9 37.9 %all-reduce.2 = (f32[18,512]{1,0:T(8,128)}, f32[512]{0:T(512)}, f32[512]{0:T(512)}) all-reduce(f32[18,512]{1,0:T(8,128)S(1)} %fusion.33, f32[512]{0:T(512)S(1)} %get-tuple-element.148, f32[512]{0:T(512)S(1)} %get-tuple-element.151), channel_id=1, replica_groups=mesh['gx'=16,'gy'=2] {'gx','gy'}, use_global_device_ids=true, to_apply=%region_22.23 | all-reduce | flops 10240 | bytes 81920 | tf_op jit(solution)/shard_map/psum | solution.py:274
  1331.0 32.4 %all-reduce.16.cloned.1.call-done = f32[1024,512]{1,0:T(8,128)} async-done(((f32[1024,512]{1,0:T(8,128)}), f32[1024,512]{1,0:T(8,128)}) %all-reduce.16.cloned.1.call-update) | async-done | bytes 2097168 | tf_op jit(solution)/shard_map/psum | solution.py:274
  (464 shorter events, 273.5 us)
Async XLA Ops:
  7.2 405.5 %copy-start = (bf16[512,1024]{1,0:T(8,128)(2,1)S(1)}, bf16[512,1024]{1,0:T(8,128)(2,1)}, u32[]{:S(2)}) copy-start(bf16[512,1024]{1,0:T(8,128)(2,1)} %param.36) | copy-start | bytes 3145732
  7.2 86.7 %all-gather.3.cloned.1.call-start = ((), (), s32[]{:S(2)}) async-start(), calls=%async_computation.4 | async-start | bytes 4718592 | tf_op jit(solution)/shard_map/all_gather | solution.py:221
  8.6 9.8 copy-start.17
  18.4 20.0 %copy-start.48 = (s32[384,4]{0,1:T(4,128)S(1)}, s32[384,4]{0,1:T(4,128)}, u32[]{:S(2)}) copy-start(s32[384,4]{0,1:T(4,128)} %param.23) | copy-start | bytes 18436
  93.9 65.1 %all-to-all-start = ((bf16[768,4,512]{2,1,0:T(4,128)(2,1)}), bf16[768,4,512]{2,1,0:T(4,128)(2,1)}, u32[]{:S(2)}, u32[]{:S(2)}) async-start(bf16[768,4,512]{2,1,0:T(4,128)(2,1)} %all-gather.3.cloned.1.call-done), calls=%async_computation | async-start | bytes 6291456 | tf_op jit(solution)/shard_map/all_to_all | solution.py:225
  99.5 142.6 %all-gather.5.cloned.1.call-start = ((), (), s32[]{:S(2)}) async-start(), calls=%async_computation.6 | async-start | bytes 4718592 | tf_op jit(solution)/shard_map/all_gather | solution.py:222
  100.3 304.9 %all-reduce.12.cloned.1.call-start = ((), (), s32[]{:S(2)}) async-start(), calls=%async_computation.5 | async-start | bytes 12582912 | tf_op jit(solution)/shard_map/psum | solution.py:120
  162.2 11.0 copy-start.19
  166.9 15.1 %copy-start.34 = (f32[3072]{0:T(1024)}, f32[3072]{0:T(1024)S(1)}, u32[]{:S(2)}) copy-start(f32[3072]{0:T(1024)S(1)} %div.59) | copy-start | bytes 36868
  193.5 43.5 %copy-start.30 = (bf16[256,512]{1,0:T(8,128)(2,1)S(1)}, bf16[256,512]{1,0:T(8,128)(2,1)}, u32[]{:S(2)}) copy-start(bf16[256,512]{1,0:T(8,128)(2,1)} %param.33) | copy-start | bytes 786436
  242.0 355.7 %all-reduce.14.cloned.1.call-start = ((), (), s32[]{:S(2)}) async-start(), calls=%async_computation.7 | async-start | bytes 12582912 | tf_op jit(solution)/shard_map/psum | solution.py:137
  410.5 12.2 copy-start.3
  412.7 10.0 copy-start.7
  412.7 10.0 copy-start.50
  461.0 277.1 %all-to-all-start.1 = ((f32[48,64,512]{2,0,1:T(8,128)}), f32[48,64,512]{2,0,1:T(8,128)}, u32[]{:S(2)}, u32[]{:S(2)}) async-start(f32[48,64,512]{2,0,1:T(8,128)} %copy.108), calls=%async_computation.1 | async-start | bytes 12582912 | tf_op jit(solution)/shard_map/all_to_all | solution.py:247
  710.8 19.4 %slice-start.4 = ((s8[6291456]{0:T(1024)(128)(4,1)}), s8[4194304]{0:T(1024)(128)(4,1)S(1)}, s32[]{:S(2)}) async-start(s8[6291456]{0:T(1024)(128)(4,1)} %bitcast.170), calls=%async_computation.14 | async-start | bytes 8388608
  716.4 13.8 slice-start.5
  738.1 135.6 %all-to-all-start.3 = ((f32[48,64,512]{2,0,1:T(8,128)}), f32[48,64,512]{2,0,1:T(8,128)}, u32[]{:S(2)}, u32[]{:S(2)}) async-start(f32[48,64,512]{2,0,1:T(8,128)} %copy.113), calls=%async_computation.3 | async-start | bytes 12582912 | tf_op jit(solution)/shard_map/all_to_all | solution.py:248
  743.9 587.0 %all-reduce.18.cloned.1.call-start = ((), (), s32[]{:S(2)}) async-start(), calls=%async_computation.9 | async-start | bytes 12582912 | tf_op jit(solution)/shard_map/psum | solution.py:288
  744.0 25.1 %copy-start.55 = (u32[32]{0:T(128)S(1)}, u32[32]{0:T(128)}, u32[]{:S(2)}) copy-start(u32[32]{0:T(128)} %constant.93) | copy-start | bytes 388
  744.0 26.4 %copy-start.20 = (f32[48,16,4]{2,1,0:T(8,128)S(1)}, f32[48,16,4]{2,1,0:T(8,128)}, u32[]{:S(2)}) copy-start(f32[48,16,4]{2,1,0:T(8,128)} %copy-done.19) | copy-start | bytes 36868
  744.0 26.4 %copy-start.25 = (f32[48,16,4]{2,1,0:T(8,128)S(1)}, f32[48,16,4]{2,1,0:T(8,128)}, u32[]{:S(2)}) copy-start(f32[48,16,4]{2,1,0:T(8,128)} %get-tuple-element.209) | copy-start | bytes 36868
  744.0 26.4 %copy-start.46 = (f32[512]{0:T(512)S(1)}, f32[512]{0:T(512)}, u32[]{:S(2)}) copy-start(f32[512]{0:T(512)} %param.29) | copy-start | bytes 6148
  776.0 14.3 %slice-start.2 = ((s8[6291456]{0:T(1024)(128)(4,1)}), s8[2097152]{0:T(1024)(128)(4,1)S(1)}, s32[]{:S(2)}) async-start(s8[6291456]{0:T(1024)(128)(4,1)} %bitcast.168), calls=%async_computation.12 | async-start | bytes 4194304
  781.7 8.6 slice-start.3
  781.7 8.6 copy-start.54
  790.3 9.7 copy-start.15
  805.5 557.9 %all-reduce.16.cloned.1.call-start = ((), (), s32[]{:S(2)}) async-start(), calls=%async_computation.8 | async-start | bytes 4194304 | tf_op jit(solution)/shard_map/psum | solution.py:274
  1179.2 110.2 %copy-start.41 = (s32[1536]{0:T(1024)S(1)}, s32[1536]{0:T(1024)}, u32[]{:S(2)}) copy-start(s32[1536]{0:T(1024)} %copy-done.40) | copy-start | bytes 18436
  1331.0 41.0 %copy-start.24 = (f32[512,1024]{1,0:T(8,128)S(1)}, f32[512,1024]{1,0:T(8,128)}, u32[]{:S(2)}) copy-start(f32[512,1024]{1,0:T(8,128)} %get-tuple-element.383) | copy-start | bytes 6291460
  1363.4 9.9 copy-start.23
  1363.4 11.2 copy-start.1
  (51 other events, 198.2 us)
Sparse Core Ops, SparseCore 0:
  46.2 47.6 all-gather.2
  101.9 45.2 all-gather.4
  242.1 162.9 all-reduce.11
  444.5 153.1 all-reduce.13
  805.6 207.0 all-reduce.17
  1183.9 179.4 all-reduce.15
where the time goes:
time: 1390 us; the launch traced here: 1380 us
  blocking collectives  516 us (37%)
  waiting for transfers between devices  394 us (28%)
  local copies, waits for them, and re-layouts  220 us (16%)
  matrix products  136 us (10%)
  other arithmetic  80.5 us (6%)
  starting transfers between devices  18.5 us (1%)
  between operations  16 us (1%)
    unnamed x1, blocking collectives  290 us
    psum x1, waiting for transfers between devices, layer_pass(): d_normed_two = lax.psum(d_normed_two, 'gy')  131 us
    psum x1, blocking collectives, per_device(): lax.psum((query_part, key_part, value_part, out_part_grad, second_gain_pa...  102 us
    all_to_all x1, blocking collectives, per_device(): lax.all_to_all(cot_all, 'gx', split_axis=0, concat_axis=1, tiled=True)  85.4 us
    psum x1, waiting for transfers between devices, layer_pass(): branch = lax.psum(branch, 'gy')  67 us
    all_to_all x1, waiting for transfers between devices, per_device(): lax.all_to_all(grad_seq, 'gx', split_axis=1, concat_axis=0, tiled=True)  58.3 us
    all_to_all x1, waiting for transfers between devices, per_device(): lax.all_to_all(token_all, 'gx', split_axis=0, concat_axis=1, tiled=True)  57.1 us
    all_gather x1, waiting for transfers between devices, per_device(): lax.all_gather(tokens, 'gy', axis=0, tiled=True)  47.8 us
  transfers between devices with their start and end apart: 9, of which 6 were waited for; matrix products, arithmetic and copies ran while one was open for 24% of the time, Pallas kernels for 0%

commit v1 on v0

--- a/solution.py
+++ b/solution.py
@@ -272,7 +272,7 @@
         down_bias_part,
     ) = parts
     stem_grad, action_grad, first_gain_grad, first_bias_grad = lax.psum(
-        (stem_part, action_part, first_gain_part, first_bias_part), ("gx", "gy")
+        lax.psum((stem_part, action_part, first_gain_part, first_bias_part), "gy"), axis_name="gx"
     )
     (
         query_grad,

time: 1390 us -> 1400 us (level)
  blocking collectives: 516 us -> 443 us
  waiting for transfers between devices: 394 us -> 436 us
  starting transfers between devices: 18.5 us -> 40.2 us
    psum x2 -> x1, blocking collectives: 140 us -> 61.1 us  [per_device(): lax.psum(lax.psum((stem_part, action_part, first_gain_part, first_bias_pa...]
    psum x1, waiting for transfers between devices: 131 us -> 153 us  [layer_pass(): d_normed_two = lax.psum(d_normed_two, 'gy')]
    all_to_all x1, starting transfers between devices: 6.08 us -> 28.1 us  [per_device(): lax.all_to_all(out_seq, 'gx', split_axis=1, concat_axis=0, tiled=True)]
    all_to_all x1, waiting for transfers between devices: 58.3 us -> 72.7 us  [per_device(): lax.all_to_all(grad_seq, 'gx', split_axis=1, concat_axis=0, tiled=True)]
    unnamed x1 -> x2, blocking collectives: 290 us -> 297 us
  transfers between devices with their start and end apart: 9 -> 9, of which waited for: 6 -> 6; matrix products, arithmetic and copies ran while one was open for 24% -> 15% of each run, Pallas kernels for 0% -> 0%
where the time goes in v1:
time: 1400 us; the launch traced here: 1390 us
  blocking collectives  443 us (32%)
  waiting for transfers between devices  436 us (31%)
  local copies, waits for them, and re-layouts  228 us (16%)
  matrix products  143 us (10%)
  other arithmetic  81.1 us (6%)
  starting transfers between devices  40.2 us (3%)
  between operations  15.7 us (1%)
    unnamed x2, blocking collectives  297 us
    psum x1, waiting for transfers between devices, layer_pass(): d_normed_two = lax.psum(d_normed_two, 'gy')  153 us
    all_to_all x1, blocking collectives, per_device(): lax.all_to_all(cot_all, 'gx', split_axis=0, concat_axis=1, tiled=True)  85.5 us
    all_to_all x1, waiting for transfers between devices, per_device(): lax.all_to_all(grad_seq, 'gx', split_axis=1, concat_axis=0, tiled=True)  72.7 us
    psum x1, waiting for transfers between devices, layer_pass(): branch = lax.psum(branch, 'gy')  66.8 us
    psum x1, blocking collectives, per_device(): lax.psum(lax.psum((stem_part, action_part, first_gain_part, first_bias_pa...  61.1 us
    all_to_all x1, waiting for transfers between devices, per_device(): lax.all_to_all(token_all, 'gx', split_axis=0, concat_axis=1, tiled=True)  57.5 us
    all_gather x1, waiting for transfers between devices, per_device(): lax.all_gather(tokens, 'gy', axis=0, tiled=True)  47.8 us
  transfers between devices with their start and end apart: 9, of which 6 were waited for; matrix products, arithmetic and copies ran while one was open for 15% of the time, Pallas kernels for 0%

profile of v1, /device:TPU:0, one launch (start us, length us, event | category | flops | bytes accessed | tf_op | source)
XLA Modules:
  0.0 1388.6 jit_solution(12989979130121625153)
XLA Ops:
  9.6 9.8 eq.86
  19.4 19.9 %eq.87 = s32[1536,1024]{1,0:T(8,128)} reshape(s32[384,4,32,32]{3,2,1,0:T(8,128)} %eq.86) | data formatting | bytes 12582912 | tf_op jit(solution)/shard_map/eq | solution.py:210
  46.7 47.8 %all-gather.3.cloned.1.call-done = bf16[768,4,512]{2,1,0:T(4,128)(2,1)} async-done(((bf16[384,4,512]{2,1,0:T(4,128)(2,1)}), bf16[768,4,512]{2,1,0:T(4,128)(2,1)}) %all-gather.3.cloned.1.call-update) | async-done | bytes 3145744 | tf_op jit(solution)/shard_map/all_gather | solution.py:221
  102.2 57.5 %all-to-all-done = bf16[768,4,512]{2,1,0:T(4,128)(2,1)} async-done(((bf16[768,4,512]{2,1,0:T(4,128)(2,1)}), bf16[768,4,512]{2,1,0:T(4,128)(2,1)}, u32[]{:S(2)}, u32[]{:S(2)}) %all-to-all-start) | async-done | bytes 3145760 | tf_op jit(solution)/shard_map/all_to_all | solution.py:225
  167.4 6.3 copy_bitcast_fusion
  174.8 7.7 reshape.397
  194.0 45.5 %while.24 = (s32[]{:T(128)}, bf16[6,8,64,256]{3,2,1,0:T(8,128)(2,1)}, bf16[6,8,64,256]{3,2,1,0:T(8,128)(2,1)}, s32[6,8,64]{2,1,0:T(8,128)S(1)}, bf16[6,8,64,256]...) while((s32[]{:T(128)}, bf16[6,8,64,256]{3,2,1,0:T(8,128)(2,1)}, ...), condition=%wide.region_5.6_spmd, body=%wide.region_2.5_spmd.sunk | while | flops 34674816 | bytes 9009281 | solution.py:115
  244.6 85.5 %all_to_all.60 = bf16[768,4,512]{2,1,0:T(4,128)(2,1)S(1)} all-to-all(bf16[768,4,512]{2,1,0:T(4,128)(2,1)} %all-gather.5.cloned.1.call-done), channel_id=1, replica_groups=mesh['gx'=16,'gy'=2] {'gx'}, dimensions={0} | all-to-all | bytes 6291456 | tf_op jit(solution)/shard_map/all_to_all | solution.py:226
  340.9 66.8 %all-reduce.12.cloned.1.call-done = f32[3072,512]{1,0:T(8,128)} async-done(((f32[3072,512]{1,0:T(8,128)}), f32[3072,512]{1,0:T(8,128)}) %all-reduce.12.cloned.1.call-update) | async-done | bytes 6291472 | tf_op jit(solution)/shard_map/psum | solution.py:120
  415.3 9.9 multiply_convert_fusion
  425.1 13.3 convert_reduce_fusion
  441.1 5.8 fusion.47
  446.9 153.4 %all-reduce.14.cloned.1.call-done = f32[3072,512]{1,0:T(8,128)} async-done(((f32[3072,512]{1,0:T(8,128)}), f32[3072,512]{1,0:T(8,128)}) %all-reduce.14.cloned.1.call-update) | async-done | bytes 6291472 | tf_op jit(solution)/shard_map/psum | solution.py:137
  600.3 6.1 multiply_reduce_fusion
  621.0 100.7 %while.25 = (s32[]{:T(128)}, bf16[6,8,64,256]{3,2,1,0:T(8,128)(2,1)}, bf16[6,8,64,256]{3,2,1,0:T(8,128)(2,1)}, bf16[6,8,64,256]{3,2,1,0:T(8,128)(2,1)}, bf16[6,8...) while((s32[]{:T(128)}, ...), condition=%wide.region_17.18_spmd, body=%wide.region_13.17_spmd.sunk | while | flops 86839424 | bytes 17954980 | solution.py:144
  730.0 8.3 multiply_reduce_fusion.1
  745.5 6.2 copy.113
  757.6 9.9 iota_compare_fusion.2
  767.5 15.2 %eq.98 = pred[1536,1024]{1,0:T(32,128)(4,1)} reshape(pred[384,4,32,32]{3,2,1,0:T(32,128)(4,1)} %iota_compare_fusion.2) | data formatting | bytes 3145728 | tf_op jit(solution)/shard_map/eq | solution.py:210
  783.9 8.8 multiply_add_fusion
  792.7 6.4 copy.108
  799.1 72.7 %all-to-all-done.3 = f32[48,64,512]{2,0,1:T(8,128)} async-done(((f32[48,64,512]{2,0,1:T(8,128)}), f32[48,64,512]{2,0,1:T(8,128)}, u32[]{:S(2)}, u32[]{:S(2)}) %all-to-all-start.3) | async-done | bytes 6291488 | tf_op jit(solution)/shard_map/all_to_all | solution.py:248
  871.7 28.1 %all-to-all-start.1 = ((f32[48,64,512]{2,0,1:T(8,128)}), f32[48,64,512]{2,0,1:T(8,128)}, u32[]{:S(2)}, u32[]{:S(2)}) async-start(f32[48,64,512]{2,0,1:T(8,128)} %copy.108), calls=%async_computation.1 | async-start | bytes 12582912 | tf_op jit(solution)/shard_map/all_to_all | solution.py:247
  899.9 6.0 add_convert_fusion
  914.7 9.5 fusion.39
  924.2 9.6 copy.114
  933.8 148.2 %all-reduce.19 = bf16[768,4,512]{2,1,0:T(4,128)(2,1)} all-reduce(f32[768,4,512]{2,1,0:T(4,128)} %bitcast.175), channel_id=3, replica_groups=mesh['gx'=16,'gy'=2] {'gy'}, use_global_device_ids=true, to_apply=%region_20.21.clone | all-reduce | flops 1572864 | bytes 9437184
  1093.9 8.6 fusion.55
  1109.8 9.7 copy.109
  1120.2 37.2 %all-reduce.16.cloned.1.call-done = f32[1024,512]{1,0:T(8,128)} async-done(((f32[1024,512]{1,0:T(8,128)}), f32[1024,512]{1,0:T(8,128)}) %all-reduce.16.cloned.1.call-update) | async-done | bytes 2097168 | tf_op jit(solution)/shard_map/psum | solution.py:275
  1157.4 148.7 %all-reduce.20 = (bf16[768,4,512]{2,1,0:T(4,128)(2,1)}, f32[18,512]{1,0:T(8,128)S(1)}, f32[512]{0:T(512)S(1)}, f32[512]{0:T(512)S(1)}) all-reduce(f32[768,4,512]{2,1,0:T(4,128)} %bitcast.174, f32[18,512]{1,0:T(8,128)S(1)} %fusion.33, f32[512]{0:T(512)S(1)} %get-tuple-element.148, ...), channel_id=2, replica_groups=mesh['gx'=16,'gy'=2] {'gy'}, use_global_device_ids=true, to_apply=%region_9.10.clone | all-reduce | flops 1583104 | bytes 9519104
  1306.1 61.1 %all-reduce.2 = (f32[18,512]{1,0:T(8,128)}, f32[512]{0:T(512)}, f32[512]{0:T(512)}, f32[512]{0:T(512)}, f32[512]{0:T(512)}, /*index=5*/f32[1024]{0:T(1024)}, f32[512]{0:T(512)}) all-reduce(f32[18,512]{1,0:T(8,128)S(1)} %get-tuple-element.197, f32[512]{0:T(512)S(1)} %get-tuple-element.198, ...), channel_id=1, replica_groups=mesh['gx'=16,'gy'=2] {'gx'}, use_global_device_ids=true, to_apply=%region_24.25 | all-reduce | flops 12800 | bytes 102400 | tf_op jit(solution)/shard_map/psum | solution.py:274
  (459 shorter events, 287.9 us)
Async XLA Ops:
  7.2 408.0 %copy-start = (bf16[512,1024]{1,0:T(8,128)(2,1)S(1)}, bf16[512,1024]{1,0:T(8,128)(2,1)}, u32[]{:S(2)}) copy-start(bf16[512,1024]{1,0:T(8,128)(2,1)} %param.36) | copy-start | bytes 3145732
  7.2 87.3 %all-gather.3.cloned.1.call-start = ((), (), s32[]{:S(2)}) async-start(), calls=%async_computation.4 | async-start | bytes 4718592 | tf_op jit(solution)/shard_map/all_gather | solution.py:221
  8.4 35.8 %copy-start.41 = (s32[1536]{0:T(1024)}, s32[1536]{0:T(1024)S(1)}, u32[]{:S(2)}) copy-start(s32[1536]{0:T(1024)S(1)} %eq.92) | copy-start | bytes 18436
  9.6 9.8 copy-start.16
  94.5 65.1 %all-to-all-start = ((bf16[768,4,512]{2,1,0:T(4,128)(2,1)}), bf16[768,4,512]{2,1,0:T(4,128)(2,1)}, u32[]{:S(2)}, u32[]{:S(2)}) async-start(bf16[768,4,512]{2,1,0:T(4,128)(2,1)} %all-gather.3.cloned.1.call-done), calls=%async_computation | async-start | bytes 6291456 | tf_op jit(solution)/shard_map/all_to_all | solution.py:225
  100.2 144.4 %all-gather.5.cloned.1.call-start = ((), (), s32[]{:S(2)}) async-start(), calls=%async_computation.6 | async-start | bytes 4718592 | tf_op jit(solution)/shard_map/all_gather | solution.py:222
  100.9 306.8 %all-reduce.12.cloned.1.call-start = ((), (), s32[]{:S(2)}) async-start(), calls=%async_computation.5 | async-start | bytes 12582912 | tf_op jit(solution)/shard_map/psum | solution.py:120
  162.8 10.9 copy-start.19
  163.1 19.4 %copy-start.35 = (f32[3072]{0:T(1024)}, f32[3072]{0:T(1024)S(1)}, u32[]{:S(2)}) copy-start(f32[3072]{0:T(1024)S(1)} %div.59) | copy-start | bytes 36868
  194.0 45.5 %copy-start.30 = (bf16[256,512]{1,0:T(8,128)(2,1)S(1)}, bf16[256,512]{1,0:T(8,128)(2,1)}, u32[]{:S(2)}) copy-start(bf16[256,512]{1,0:T(8,128)(2,1)} %param.33) | copy-start | bytes 786436
  244.5 355.7 %all-reduce.14.cloned.1.call-start = ((), (), s32[]{:S(2)}) async-start(), calls=%async_computation.7 | async-start | bytes 12582912 | tf_op jit(solution)/shard_map/psum | solution.py:137
  413.0 12.1 copy-start.3
  415.2 9.9 copy-start.7
  415.2 9.9 copy-start.50
  621.0 100.7 %copy-start.32 = (bf16[512,256]{1,0:T(8,128)(2,1)S(1)}, bf16[512,256]{1,0:T(8,128)(2,1)}, u32[]{:S(2)}) copy-start(bf16[512,256]{1,0:T(8,128)(2,1)} %param.31) | copy-start | bytes 786436
  724.3 19.3 %slice-start.2 = ((s8[6291456]{0:T(1024)(128)(4,1)}), s8[4194304]{0:T(1024)(128)(4,1)S(1)}, s32[]{:S(2)}) async-start(s8[6291456]{0:T(1024)(128)(4,1)} %bitcast.168), calls=%async_computation.12 | async-start | bytes 8388608
  730.0 13.7 slice-start.3
  751.7 120.0 %all-to-all-start.3 = ((f32[48,64,512]{2,0,1:T(8,128)}), f32[48,64,512]{2,0,1:T(8,128)}, u32[]{:S(2)}, u32[]{:S(2)}) async-start(f32[48,64,512]{2,0,1:T(8,128)} %copy.113), calls=%async_computation.3 | async-start | bytes 12582912 | tf_op jit(solution)/shard_map/all_to_all | solution.py:248
  757.5 25.1 %copy-start.55 = (u32[32]{0:T(128)S(1)}, u32[32]{0:T(128)}, u32[]{:S(2)}) copy-start(u32[32]{0:T(128)} %constant.93) | copy-start | bytes 388
  757.5 26.4 %copy-start.52 = (f32[512]{0:T(512)S(1)}, f32[512]{0:T(512)}, u32[]{:S(2)}) copy-start(f32[512]{0:T(512)} %param.39) | copy-start | bytes 6148
  799.0 100.8 %copy-start.20 = (f32[48,16,4]{2,1,0:T(8,128)S(1)}, f32[48,16,4]{2,1,0:T(8,128)}, u32[]{:S(2)}) copy-start(f32[48,16,4]{2,1,0:T(8,128)} %copy-done.19) | copy-start | bytes 36868
  799.0 100.8 %copy-start.25 = (f32[48,16,4]{2,1,0:T(8,128)S(1)}, f32[48,16,4]{2,1,0:T(8,128)}, u32[]{:S(2)}) copy-start(f32[48,16,4]{2,1,0:T(8,128)} %get-tuple-element.212) | copy-start | bytes 36868
  799.0 100.9 %copy-start.47 = (f32[512]{0:T(512)S(1)}, f32[512]{0:T(512)}, u32[]{:S(2)}) copy-start(f32[512]{0:T(512)} %param.29) | copy-start | bytes 6148
  871.7 238.1 %all-to-all-start.1 = ((f32[48,64,512]{2,0,1:T(8,128)}), f32[48,64,512]{2,0,1:T(8,128)}, u32[]{:S(2)}, u32[]{:S(2)}) async-start(f32[48,64,512]{2,0,1:T(8,128)} %copy.108), calls=%async_computation.1 | async-start | bytes 12582912 | tf_op jit(solution)/shard_map/all_to_all | solution.py:247
  899.8 257.6 %all-reduce.16.cloned.1.call-start = ((), (), s32[]{:S(2)}) async-start(), calls=%async_computation.8 | async-start | bytes 4194304 | tf_op jit(solution)/shard_map/psum | solution.py:275
  905.9 8.8 copy-start.54
  1093.7 276.7 %all-reduce.18.cloned.1.call-start = ((), (), s32[]{:S(2)}) async-start(), calls=%async_computation.9 | async-start | bytes 16777216 | tf_op jit(solution)/shard_map/psum | solution.py:274
  1109.8 9.7 copy-start.18
  1109.8 9.7 copy-start.42
  1157.4 148.7 %copy-start.49 = (f32[1024]{0:T(1024)S(1)}, f32[1024]{0:T(1024)}, u32[]{:S(2)}) copy-start(f32[1024]{0:T(1024)} %get-tuple-element.217) | copy-start | bytes 12292
  1370.3 9.9 copy-start.23
  1370.4 11.2 copy-start.1
  (49 other events, 195.3 us)
Sparse Core Ops, SparseCore 0:
  46.8 47.6 all-gather.2
  102.6 45.2 all-gather.4
  244.7 163.0 all-reduce.11
  447.0 153.1 all-reduce.13
  1093.8 63.5 all-reduce.15
  1163.8 172.7 all-reduce.17
